TPU v7x, 256 devices: a whole 4x4x8 slice. The times are simulated.
256 devices in a mesh: dp: 16 (over z, core), expert: 4 (over y), blk: 4 (over x).
Axes of the slice: x: 4, y: 4, z: 8, core: 2. Of those that a mesh axis runs over, the one named last changes fastest.
Arguments:
- tokens: bfloat16 [2048, 6144], P('dp', 'blk'), may hold values from -6 to 6
- expert_ids: int32 [2048, 2], P('dp'), may hold values from 0 to 7, all different within a row; in each aligned block of 128 rows (0 to 127, 128 to 255, ...) at most 48 rows name the same one
- route_weights: float32 [2048, 2], P('dp'), may hold values from 0.1 to 1
- gate_weight: bfloat16 [8, 6144, 8192], P('expert', 'blk', 'dp'), may hold values from -0.078125 to 0.078125
- up_weight: bfloat16 [8, 6144, 8192], P('expert', 'blk', 'dp'), may hold values from -0.078125 to 0.078125
- down_weight: bfloat16 [8, 8192, 6144], P('expert', 'dp', 'blk'), may hold values from -0.0625 to 0.0625
Outputs:
- mixed: bfloat16 [2048, 6144], P('dp', 'blk')
Inputs may be any that keep to these rules, and one draw needn't show every extreme that they name: `expert_ids`: each row names 2 different experts. Among the 128 rows of one data shard no expert is named more than 48 times, and in every draw some expert is named exactly 48 times in some shard.
All inputs are finite; a program needn't handle non-finite values.
Results may differ from a plain program's by a relative error of at most 0.0051.
Values may be sent and summed in bfloat16 or wider, within the bound.
A program may use at most 64 MiB of HBM per device.

v0:
```python
import jax
import jax.numpy as jnp
from jax import lax
from jax.sharding import PartitionSpec as P

EXPERTS = 8
CAP = 48


def local(tokens, expert_ids, route_weights, gate_weight, up_weight, down_weight):
    local_count = gate_weight.shape[0]
    token_count = tokens.shape[0]
    top_count = expert_ids.shape[1]
    group_index = lax.axis_index("expert")
    flat_ids = expert_ids.reshape(-1)
    one_hot = (flat_ids[:, None] == jnp.arange(EXPERTS, dtype=jnp.int32)[None, :]).astype(jnp.int32)
    before = jnp.cumsum(one_hot, axis=0) - one_hot
    position = jnp.sum(before * one_hot, axis=1)
    local_ids = flat_ids - group_index * local_count
    is_mine = local_ids[:, None] == jnp.arange(local_count, dtype=jnp.int32)[None, :]
    in_slot = position[:, None] == jnp.arange(CAP, dtype=jnp.int32)[None, :]
    slot_hit = (is_mine[:, :, None] & in_slot[:, None, :]).reshape(
        token_count, top_count, local_count, CAP
    )
    dispatch = jnp.any(slot_hit, axis=1).astype(jnp.bfloat16)
    combine = jnp.sum(slot_hit.astype(jnp.float32) * route_weights[:, :, None, None], axis=1)
    picked = jnp.einsum("tec,tf->ecf", dispatch, tokens, preferred_element_type=jnp.float32).astype(
        jnp.bfloat16
    )
    shard_rows = lax.all_gather(picked, "dp", axis=1, tiled=True)
    gate_part = jnp.einsum(
        "enf,efh->enh", shard_rows, gate_weight, preferred_element_type=jnp.float32
    )
    up_part = jnp.einsum("enf,efh->enh", shard_rows, up_weight, preferred_element_type=jnp.float32)
    partial_value = jnp.stack([gate_part, up_part])
    summed = lax.psum(partial_value, "blk")
    hidden = (jax.nn.silu(summed[0]) * summed[1]).astype(jnp.bfloat16)
    expert_out = lax.psum_scatter(
        jnp.einsum("enh,ehd->ned", hidden, down_weight, preferred_element_type=jnp.float32),
        "dp",
        scatter_dimension=0,
        tiled=True,
    )
    mixed_part = jnp.einsum("tec,ced->td", combine, expert_out, precision=lax.Precision.HIGHEST)
    mixed = lax.psum(mixed_part, "expert")
    return mixed.astype(jnp.bfloat16)


def solution(mesh):
    placed = (
        P("dp", "blk"),
        P("dp", None),
        P("dp", None),
        P("expert", "blk", "dp"),
        P("expert", "blk", "dp"),
        P("expert", "dp", "blk"),
    )
    return jax.shard_map(
        local, mesh=mesh, in_specs=placed, out_specs=P("dp", "blk"), check_vma=False
    )
```

profile of v0, /device:TPU:1, one launch (start us, length us, event | category | flops | bytes accessed | tf_op | source)
XLA Modules:
  0.0 311.4 jit_solution(18314517861227424447)
XLA Ops:
  6.5 0.0 copy-start
  6.5 0.0 all-gather.2.cloned.1.call-start
  6.5 0.9 copy.13
  7.5 0.1 eq.65
  7.6 0.1 reshape.70
  7.8 0.6 reduce-window.6
  8.4 0.2 slice_reduce_fusion
  8.6 0.1 fusion.7
  8.7 0.1 eq.69
  8.9 0.1 copy.15
  9.0 0.7 broadcast_subtract_fusion
  9.7 1.9 convolution_convert_fusion
  11.6 0.0 all-gather.2.cloned.1.call-update
  11.6 0.0 all-reduce.3.cloned.1.call-start
  11.7 47.1 %all-gather.2.cloned.1.call-done = bf16[2,768,1536]{2,1,0:T(8,128)(2,1)} async-done(((bf16[2,48,1536]{2,1,0:T(8,128)(2,1)}), bf16[2,768,1536]{2,1,0:T(8,128)(2,1)}) %all-gather.2.cloned.1.call-update) | async-done | bytes 4718608 | tf_op jit(solution)/shard_map/all_gather | solution.py:30
  58.8 0.0 copy-start.2
  58.8 0.0 copy-start.3
  58.8 5.5 %convolution_bitcast_fusion.2 = f32[1,2,768,512]{3,2,1,0:T(8,128)S(1)} fusion(bf16[2,768,1536]{2,1,0:T(8,128)(2,1)} %all-gather.2.cloned.1.call-done, bf16[2,1536,512]{2,1,0:T(8,128)(2,1)} %param.10), kind=kOutput, calls=%fused_computation.8 | convolution fusion | flops 2415919104 | bytes 11010048 | tf_op jit(solution)/shard_map/enf,efh->enh/dot_general | solution.py:34
  64.3 0.0 copy-done.2
  64.3 0.1 copy-done.3
  64.4 2.6 convolution_bitcast_fusion.3
  67.0 3.4 %pad_maximum_fusion = f32[2,2,768,512]{3,2,1,0:T(8,128)} fusion(f32[1,2,768,512]{3,2,1,0:T(8,128)S(1)} %convolution_bitcast_fusion.2, f32[1,2,768,512]{3,2,1,0:T(8,128)S(1)} %convolution_bitcast_fusion.3), kind=kLoop, calls=%fused_computation | loop fusion | flops 1572864 | bytes 12582912 | tf_op jit(solution)/shard_map/stack | solution.py:35
  70.4 0.0 all-reduce.3.cloned.1.call-update
  70.4 0.0 reduce-scatter.2.cloned.1.call-start
  70.5 130.3 %all-reduce.3.cloned.1.call-done = f32[2,2,768,512]{3,2,1,0:T(8,128)} async-done(((f32[2,2,768,512]{3,2,1,0:T(8,128)}), f32[2,2,768,512]{3,2,1,0:T(8,128)}) %all-reduce.3.cloned.1.call-update) | async-done | bytes 6291472 | tf_op jit(solution)/shard_map/psum | solution.py:36
  200.7 0.0 copy-done
  200.7 8.0 %convolution_bitcast_fusion = f32[768,2,1536]{2,0,1:T(8,128)} fusion(bf16[2,512,1536]{2,1,0:T(8,128)(2,1)S(1)} %copy-done, f32[2,2,768,512]{3,2,1,0:T(8,128)} %all-reduce.3.cloned.1.call-done), kind=kOutput, calls=%fused_computation.1 | convolution fusion | flops 2420637696 | bytes 18874368 | tf_op jit(solution)/shard_map/enh,ehd->ned/dot_general | solution.py:39
  208.8 0.0 reduce-scatter.2.cloned.1.call-update
  208.8 0.7 copy-done.1
  209.5 69.2 %reduce-scatter.2.cloned.1.call-done = f32[48,2,1536]{2,0,1:T(8,128)} async-done(((f32[768,2,1536]{2,0,1:T(8,128)}), f32[48,2,1536]{2,0,1:T(8,128)}) %reduce-scatter.2.cloned.1.call-update) | async-done | bytes 589840 | tf_op jit(solution)/shard_map/reduce_scatter | solution.py:38
  278.7 2.8 convolution_bitcast_fusion.1
  281.5 23.4 %all-reduce.4 = bf16[128,1536]{1,0:T(8,128)(2,1)} all-reduce(f32[128,1536]{1,0:T(8,128)} %convolution_bitcast_fusion.1), channel_id=1, replica_groups=mesh['dp'=16,'expert'=4,'blk'=4] {'expert'}, use_global_device_ids=true, to_apply=%region_7.8 | all-reduce | flops 196608 | bytes 1179648 | tf_op jit(solution)/shard_map/psum | solution.py:45
  (8 shorter events, 0.1 us)
Async XLA Ops:
  6.5 194.2 %copy-start = (bf16[2,512,1536]{2,1,0:T(8,128)(2,1)S(1)}, bf16[2,512,1536]{2,1,0:T(8,128)(2,1)}, u32[]{:S(2)}) copy-start(bf16[2,512,1536]{2,1,0:T(8,128)(2,1)} %param.11) | copy-start | bytes 9437188
  6.5 52.2 %all-gather.2.cloned.1.call-start = ((), (), s32[]{:S(2)}) async-start(), calls=%async_computation.1 | async-start | bytes 5013504 | tf_op jit(solution)/shard_map/all_gather | solution.py:30
  11.6 189.1 %all-reduce.3.cloned.1.call-start = ((), (), s32[]{:S(2)}) async-start(), calls=%async_computation.2 | async-start | bytes 12582912 | tf_op jit(solution)/shard_map/psum | solution.py:36
  58.8 5.6 %copy-start.2 = (bf16[2,768,1536]{2,1,0:T(8,128)(2,1)S(1)}, bf16[2,768,1536]{2,1,0:T(8,128)(2,1)}, u32[]{:S(2)}) copy-start(bf16[2,768,1536]{2,1,0:T(8,128)(2,1)} %all-gather.2.cloned.1.call-done) | copy-start | bytes 14155780
  58.8 5.6 %copy-start.3 = (bf16[2,1536,512]{2,1,0:T(8,128)(2,1)S(1)}, bf16[2,1536,512]{2,1,0:T(8,128)(2,1)}, u32[]{:S(2)}) copy-start(bf16[2,1536,512]{2,1,0:T(8,128)(2,1)} %param.9) | copy-start | bytes 9437188
  70.4 208.3 %reduce-scatter.2.cloned.1.call-start = ((), (), s32[]{:S(2)}) async-start(), calls=%async_computation.3 | async-start | bytes 10027008 | tf_op jit(solution)/shard_map/reduce_scatter | solution.py:38
  208.8 0.7 copy-start.1
Sparse Core Ops, SparseCore 0:
  11.8 46.9 all-gather.1
  70.5 130.1 all-reduce.2
  208.9 69.7 reduce-scatter.1
where the time goes:
time: 316 us; the launch traced here: 311 us
  waiting for transfers between devices  247 us (78%)
  blocking collectives  23.4 us (7%)
  matrix products  20.9 us (7%)
  between operations  13.2 us (4%)
  other arithmetic  4.85 us (2%)
    psum x1, waiting for transfers between devices, local(): summed = lax.psum(partial_value, 'blk')  130 us
    reduce_scatter x1, waiting for transfers between devices, local(): lax.psum_scatter(jnp.einsum('enh,ehd->ned', hidden, down_weight, preferre...  69.2 us
    all_gather x1, waiting for transfers between devices, local(): shard_rows = lax.all_gather(picked, 'dp', axis=1, tiled=True)  47.1 us
    psum x1, blocking collectives, local(): mixed = lax.psum(mixed_part, 'expert')  23.4 us
    dot_general x1, matrix products, local(): jnp.einsum('enh,ehd->ned', hidden, down_weight, preferred_element_type=jn...  8.04 us
  transfers between devices with their start and end apart: 3, of which 3 were waited for; matrix products, arithmetic and copies ran while one was open for 0% of the time, Pallas kernels for 0%

commit v1 on v0

v1 whole, which is shorter than its diff:
```python
import functools

import jax
import jax.numpy as jnp
from jax import lax
from jax.experimental import pallas as pl
from jax.experimental.pallas import tpu as pltpu
from jax.sharding import PartitionSpec as P

MESH = pl.DeviceIdType.MESH
CAP = 48
NZ, NY, NX = 8, 4, 4
UNITS = 16
SUB = 2
L2, L3, L5, L6 = 2, 4, 6, 8
LC0, LC1 = 12, 16
SLOTS = LC1 + 8

F32, BF16 = jnp.float32, jnp.bfloat16


def dot(a, b, precision=None):
    return lax.dot_general(
        a, b, (((1,), (0,)), ((), ())), precision=precision, preferred_element_type=F32
    )


def slot_hits(ids, expert_of, slot_of):
    rows, lanes = ids.shape[0], slot_of.shape[1]
    first = jnp.broadcast_to(ids[:, 0:1], (rows, lanes)) == expert_of
    second = jnp.broadcast_to(ids[:, 1:2], (rows, lanes)) == expert_of
    named = jnp.where(first | second, 1.0, 0.0)
    earlier = lax.broadcasted_iota(jnp.int32, (rows, rows), 1) < lax.broadcasted_iota(
        jnp.int32, (rows, rows), 0
    )
    position = dot(jnp.where(earlier, 1.0, 0.0).astype(BF16), named.astype(BF16))
    here = position == slot_of.astype(F32)
    return first, second, jnp.where(here, named, 0.0)


def kernel(
    tok_ref, ids_ref, rw_ref, wg_hbm, wu_hbm, wd_hbm, out_ref,
    wg, wu, wd, xs, part, s_out, r_opp, r_sum, hid, own, pair_out, pair_in,
    c_out, c_in, eo0, eo1, comb,
    w_sem, a_ss, a_rs, p_ss, p_rs, x_ss, x_rs, q_ss, q_rs, c_ss, c_rs, y_ss, y_rs,
):
    dp, y, x = lax.axis_index("dp"), lax.axis_index("expert"), lax.axis_index("blk")
    z, c = dp // 2, dp % 2
    width = tok_ref.shape[1]
    sub_w = width // SUB
    partner = (z * 2 + (1 - c), y, x)
    right, left = (dp, y, (x + 1) % NX), (dp, y, (x + NX - 1) % NX)
    q_right, q_left, q_far = (x + 1) % NX, (x + NX - 1) % NX, (x + 2) % NX

    def zdev(step):
        return (((z + step + NZ) % NZ) * 2 + c, y, x)

    def ydev(step):
        return (dp, (y + step) % NY, x)

    def zchip(i):
        k = (i + 1) // 2
        return (z + k * (1 - 2 * (i % 2)) + NZ) % NZ

    def remote(src, dst, ss, rs, dev):
        return pltpu.make_async_remote_copy(
            src_ref=src, dst_ref=dst, send_sem=ss, recv_sem=rs, device_id=dev, device_id_type=MESH
        )

    weights = [
        pltpu.make_async_copy(h.at[e], v.at[e], w_sem.at[n, e])
        for e in range(2)
        for n, (h, v) in enumerate(((wg_hbm, wg), (wu_hbm, wu), (wd_hbm, wd)))
    ]
    for w in weights:
        w.start()

    barrier = pltpu.get_barrier_semaphore()
    peers = [partner, zdev(1), zdev(-1), right, left, ydev(1), ydev(2), ydev(3)]
    for d in peers:
        pl.semaphore_signal(barrier, inc=1, device_id=d, device_id_type=MESH)

    ids = ids_ref[...]
    lane = lax.broadcasted_iota(jnp.int32, (128, 128), 1)
    for e in range(2):
        _, _, hit = slot_hits(ids, 2 * y + e, lane)
        rows = lax.dot_general(
            hit.astype(BF16), tok_ref[...], (((0,), (0,)), ((), ())), preferred_element_type=F32
        )[:CAP].astype(BF16)
        for s in range(SUB):
            xs[e, s, dp] = rows[:, s * sub_w : (s + 1) * sub_w]
    pl.semaphore_wait(barrier, len(peers))

    def a_copy(e, s, chip, i, step):
        at = xs.at[e, s, 2 * chip + c]
        return remote(at, at, a_ss.at[e, i, s], a_rs.at[e, i, s], zdev(step))

    def p_copy(e, s, chip, i, core):
        at = xs.at[e, s, 2 * chip + core]
        return remote(at, at, p_ss.at[e, i, s], p_rs.at[e, i, s], partner)

    def send_own(e):
        for s in range(SUB):
            a_copy(e, s, z, 1, 1).start()
            a_copy(e, s, z, 2, -1).start()
            p_copy(e, s, z, 0, c).start()

    def pass_on(t):
        e, m = t // 4, t % 4
        for s in range(SUB):
            i = 2 * m + 1
            chip = zchip(i)
            a_copy(e, s, chip, i, 1).wait_recv()

            @pl.when((m < 2) | ((m == 2) & (e == 0)))
            def _():
                a_copy(e, s, chip, i + 2, 1).start()

            p_copy(e, s, chip, i, c).start()

            @pl.when(m < 3)
            def _():
                i = 2 * m + 2
                chip = zchip(i)
                a_copy(e, s, chip, i, -1).wait_recv()

                @pl.when((m < 2) | (e == 1))
                def _():
                    a_copy(e, s, chip, i + 2 - i // 6, -1).start()

                p_copy(e, s, chip, i, c).start()

    def unit(u):
        e, j = u // 8, u % 8
        i0 = j + (j // 4) * (11 - 2 * j)
        i = i0 + e * (7 - j - i0)
        return e, i, e * 8 + i

    def x_copy(v, n):
        src, dst, dev = (
            lambda: (s_out.at[v, q_far, 0], r_opp.at[v, 0], right),
            lambda: (s_out.at[v, q_far, 1], r_opp.at[v, 1], left),
            lambda: (s_out.at[v, q_right, 1], r_sum.at[v, 0, 1], right),
            lambda: (s_out.at[v, q_left, 0], r_sum.at[v, 1, 0], left),
            lambda: (s_out.at[v, q_right, 0], r_sum.at[v, 0, 0], right),
            lambda: (s_out.at[v, q_left, 1], r_sum.at[v, 1, 1], left),
            lambda: (hid.at[v, x], hid.at[v, x], right),
            lambda: (hid.at[v, x], hid.at[v, x], left),
            lambda: (hid.at[v, q_left, 0], hid.at[v, q_left, 0], right),
            lambda: (hid.at[v, q_right, 1], hid.at[v, q_right, 1], left),
        )[n]()
        return remote(src, dst, x_ss.at[v, n], x_rs.at[v, n], dev)

    def x_landed(v, n):
        at = (
            r_opp.at[v, 0],
            r_opp.at[v, 1],
            r_sum.at[v, 0, 1],
            r_sum.at[v, 1, 0],
            r_sum.at[v, 0, 0],
            r_sum.at[v, 1, 1],
            hid.at[v, q_left],
            hid.at[v, q_right],
            hid.at[v, q_far, 0],
            hid.at[v, q_far, 1],
        )[n]
        remote(at, at, x_ss.at[v, n], x_rs.at[v, n], right if n % 2 else left).wait_recv()

    def first(u):
        e, i, v = unit(u)
        chip = zchip(i)

        @pl.when(u % 8 == 0)
        def _():
            pltpu.make_async_copy(wg_hbm.at[e], wg.at[e], w_sem.at[0, e]).wait()
            pltpu.make_async_copy(wu_hbm.at[e], wu.at[e], w_sem.at[1, e]).wait()

        for s in range(SUB):
            p_copy(e, s, chip, i, 1 - c).wait_recv()
        rows = [xs[e, s, pl.ds(2 * chip, 2)].reshape(2 * CAP, sub_w) for s in range(SUB)]
        for g, w in enumerate((wg, wu)):
            total = sum(dot(rows[s], w[e, s * sub_w : (s + 1) * sub_w]) for s in range(SUB))
            for q in range(NX):
                block = total[:, q * 128 : (q + 1) * 128]
                for h in range(2):
                    half = block[h * CAP : (h + 1) * CAP]
                    part[v, q, h, g] = half
                    s_out[v, q, h, g] = half.astype(BF16)
        for n in range(4):
            x_copy(v, n).start()

    def second(u):
        _, _, v = unit(u)
        x_landed(v, 0)
        s_out[v, q_right, 0] = (part[v, q_right, 0] + r_opp[v, 0].astype(F32)).astype(BF16)
        x_copy(v, 4).start()
        x_landed(v, 1)
        s_out[v, q_left, 1] = (part[v, q_left, 1] + r_opp[v, 1].astype(F32)).astype(BF16)
        x_copy(v, 5).start()

    def third(u):
        _, _, v = unit(u)
        for n in range(2, 6):
            x_landed(v, n)
        for h in range(2):
            both = part[v, x, h] + r_sum[v, 0, h].astype(F32) + r_sum[v, 1, h].astype(F32)
            gate, up = both[0], both[1]
            hid[v, x, h] = (gate / (1.0 + jnp.exp(-gate)) * up).astype(BF16)
        x_copy(v, 6).start()
        x_copy(v, 7).start()

    def fifth(u):
        _, _, v = unit(u)
        x_landed(v, 6)
        x_copy(v, 8).start()
        x_landed(v, 7)
        x_copy(v, 9).start()

    def q_copy(v):
        return remote(pair_out.at[v], pair_in.at[v], q_ss.at[v], q_rs.at[v], partner)

    def sixth(u):
        e, i, v = unit(u)

        @pl.when(u % 8 == 0)
        def _():
            pltpu.make_async_copy(wd_hbm.at[e], wd.at[e], w_sem.at[2, e]).wait()

        x_landed(v, 8)
        x_landed(v, 9)
        rows = jnp.concatenate(
            [
                jnp.concatenate([hid[v, q, h] for q in range(NX)], axis=1)
                for h in (c, 1 - c)
            ],
            axis=0,
        )
        for n in range(width // 512):
            cols = slice(n * 512, (n + 1) * 512)
            block = dot(rows, wd[e, :, cols])
            own[v, :, cols] = block[:CAP]
            pair_out[v, :, cols] = block[CAP:]
        q_copy(v).start()
        for n in range(10):
            x_copy(v, n).wait_send()

    def c_copy(e, i, step):
        v = e * 8 + i
        return remote(c_out.at[v], c_in.at[v], c_ss.at[v], c_rs.at[v], zdev(step))

    def y_copy(e, o):
        buf = (eo0, eo1)[e]
        return remote(buf.at[y], buf.at[y], y_ss.at[e, o], y_rs.at[e, o], ydev(o))

    def y_landed(e, o):
        at = (eo0, eo1)[e].at[(y + NY - o) % NY]
        remote(at, at, y_ss.at[e, o], y_rs.at[e, o], ydev(o)).wait_recv()

    def reduce_z(e, j):
        i = 7 - j
        v = e * 8 + i
        q_copy(v).wait_recv()

        def from_up(slot):
            c_copy(e, slot, 1).wait_recv()
            return c_in[e * 8 + slot].astype(F32)

        def send():
            step = 1 - 2 * (i % 2)
            c_copy(e, i, step).start()

        no_up = (j == 0) | (j == (2 if e else 1))

        @pl.when(no_up)
        def _():
            c_out[v] = (own[v] + pair_in[v]).astype(BF16)

        @pl.when((j < 7) & jnp.logical_not(no_up))
        def _():
            c_out[v] = (own[v] + pair_in[v] + from_up(i + 2 - i // 6)).astype(BF16)

        if e == 0:

            @pl.when(j < 7)
            def _():
                send()
        else:

            @pl.when(j == 0)
            def _():
                c_copy(e, 7, 1).start()

            @pl.when((j > 0) & (j < 7))
            def _():
                send()

        @pl.when(j == 7)
        def _():
            total = own[v] + pair_in[v] + from_up(1) + from_up(2)
            if e == 0:
                eo0[y] = total
            else:
                eo1[y] = total.astype(BF16)
            for o in range(1, NY):
                y_copy(e, o).start()

    send_own(0)

    lanes = NY * CAP
    slot = lax.broadcasted_iota(jnp.int32, (128, lanes), 1)
    for e in range(2):
        expert_of = 2 * (slot // CAP) + e
        one, two, hit = slot_hits(ids, expert_of, slot % CAP)
        weight = jnp.where(one, rw_ref[:, 0:1], 0.0) + jnp.where(two, rw_ref[:, 1:2], 0.0)
        comb[e] = weight * hit

    def body(t, carry):
        def within(lag, count, f):
            @pl.when((t >= lag) & (t < lag + count))
            def _():
                f(t - lag)

        within(0, UNITS, first)

        @pl.when(t == 1)
        def _():
            send_own(1)

        within(0, 8, pass_on)
        within(L6, UNITS, sixth)
        within(L5, UNITS, fifth)
        within(L3, UNITS, third)
        within(L2, UNITS, second)
        within(LC0, 8, functools.partial(reduce_z, 0))
        within(LC1, 8, functools.partial(reduce_z, 1))
        return carry

    lax.fori_loop(0, SLOTS, body, 0)

    highest = lax.Precision.HIGHEST
    for o in range(1, NY):
        y_landed(0, o)
    total = dot(comb[0], eo0[...].reshape(lanes, width), highest)

    for e in range(2):

        def sent(i, carry):
            v = e * 8 + i
            q_copy(v).wait_send()
            for s in range(SUB):
                p_copy(e, s, z, i, c).wait_send()

            @pl.when(i > 0)
            def _():
                c_copy(e, i, 1).wait_send()
                for s in range(SUB):
                    a_copy(e, s, z, i, 1).wait_send()

            return carry

        lax.fori_loop(0, 8, sent, 0)
        for o in range(1, NY):
            y_copy(e, o).wait_send()

    for o in range(1, NY):
        y_landed(1, o)
    late = eo1[...].reshape(lanes, width).astype(F32)
    out_ref[...] = (total + dot(comb[1], late, highest)).astype(BF16)


def local(tokens, expert_ids, route_weights, gate_weight, up_weight, down_weight):
    rows, width = tokens.shape
    hidden = gate_weight.shape[2]
    quarter = hidden // NX
    vmem = pl.BlockSpec(memory_space=pltpu.VMEM)
    hbm = pl.BlockSpec(memory_space=pl.ANY)
    dma = pltpu.SemaphoreType.DMA
    return pl.pallas_call(
        kernel,
        out_shape=jax.ShapeDtypeStruct((rows, width), BF16),
        in_specs=[vmem, vmem, vmem, hbm, hbm, hbm],
        out_specs=vmem,
        scratch_shapes=[
            pltpu.VMEM(gate_weight.shape, BF16),
            pltpu.VMEM(up_weight.shape, BF16),
            pltpu.VMEM(down_weight.shape, BF16),
            pltpu.VMEM((2, SUB, 2 * NZ, CAP, width // SUB), BF16),
            pltpu.VMEM((UNITS, NX, 2, 2, CAP, quarter), F32),
            pltpu.VMEM((UNITS, NX, 2, 2, CAP, quarter), BF16),
            pltpu.VMEM((UNITS, 2, 2, CAP, quarter), BF16),
            pltpu.VMEM((UNITS, 2, 2, 2, CAP, quarter), BF16),
            pltpu.VMEM((UNITS, NX, 2, CAP, quarter), BF16),
            pltpu.VMEM((UNITS, CAP, width), F32),
            pltpu.VMEM((UNITS, CAP, width), F32),
            pltpu.VMEM((UNITS, CAP, width), F32),
            pltpu.VMEM((UNITS, CAP, width), BF16),
            pltpu.VMEM((UNITS, CAP, width), BF16),
            pltpu.VMEM((NY, CAP, width), F32),
            pltpu.VMEM((NY, CAP, width), BF16),
            pltpu.VMEM((2, rows, NY * CAP), F32),
            dma((3, 2)),
            dma((2, 8, SUB)),
            dma((2, 8, SUB)),
            dma((2, 8, SUB)),
            dma((2, 8, SUB)),
            dma((UNITS, 10)),
            dma((UNITS, 10)),
            dma((UNITS,)),
            dma((UNITS,)),
            dma((UNITS,)),
            dma((UNITS,)),
            dma((2, NY)),
            dma((2, NY)),
        ],
        compiler_params=pltpu.CompilerParams(
            collective_id=0, has_side_effects=True, vmem_limit_bytes=60 * 2**20
        ),
    )(tokens, expert_ids, route_weights, gate_weight, up_weight, down_weight)


def solution(mesh):
    placed = (
        P("dp", "blk"),
        P("dp", None),
        P("dp", None),
        P("expert", "blk", "dp"),
        P("expert", "blk", "dp"),
        P("expert", "dp", "blk"),
    )
    return jax.shard_map(
        local, mesh=mesh, in_specs=placed, out_specs=P("dp", "blk"), check_vma=False
    )
```

time: 316 us -> 112 us (0.35); the launches traced: 311 us -> 112 us
  waiting for transfers between devices: 247 us -> 0 us
  Pallas kernels: 0 us -> 108 us
  blocking collectives: 23.4 us -> 0 us
  matrix products: 20.9 us -> 0 us
  between operations: 13.2 us -> 0.01 us
  other arithmetic: 4.85 us -> 0 us
    psum x1 -> x0, waiting for transfers between devices: 130 us -> none  [local(): summed = lax.psum(partial_value, 'blk')]
    pallas_call x0 -> x1, Pallas kernels: none -> 108 us  [local(): pl.pallas_call(kernel, out_shape=jax.ShapeDtypeStruct((rows, width), BF16...]
    reduce_scatter x1 -> x0, waiting for transfers between devices: 69.2 us -> none  [local(): lax.psum_scatter(jnp.einsum('enh,ehd->ned', hidden, down_weight, preferre...]
    all_gather x1 -> x0, waiting for transfers between devices: 47.1 us -> none  [local(): shard_rows = lax.all_gather(picked, 'dp', axis=1, tiled=True)]
    psum x1 -> x0, blocking collectives: 23.4 us -> none  [local(): mixed = lax.psum(mixed_part, 'expert')]
    dot_general x5 -> x0, matrix products: 20.9 us -> none  [the longest x1 8.04 us: local(): jnp.einsum('enh,ehd->ned', hidden, down_weight, preferred_element_type=jn...]
    another operation x3 -> x0, other arithmetic: 4 us -> none  [the longest x1 3.37 us: local(): partial_value = jnp.stack([gate_part, up_part])]
  transfers between devices with their start and end apart: 3 -> 0, of which waited for: 3 -> 0; matrix products, arithmetic and copies ran while one was open for 0% -> 0% of each run, Pallas kernels for 0% -> 0%
where the time goes in v1:
time: 112 us
  Pallas kernels  108 us (96%)
  local copies, waits for them, and re-layouts  4.58 us (4%)
    pallas_call x1, Pallas kernels, local(): pl.pallas_call(kernel, out_shape=jax.ShapeDtypeStruct((rows, width), BF16...  108 us
    unnamed x3, local copies, waits for them, and re-layouts  4.58 us

profile of v1, /device:TPU:1, one launch (start us, length us, event | category | flops | bytes accessed | tf_op | source)
XLA Modules:
  0.0 112.3 jit_solution(18233741401022976963)
XLA Ops:
  0.0 1.4 %copy.7.ids_ref = s32[128,2]{1,0:T(8,128)} copy(s32[128,2]{0,1:T(2,128)} %param.7) | data formatting | bytes 2048 | tf_op args[1]
  1.4 1.4 %copy.8.rw_ref = f32[128,2]{1,0:T(8,128)} copy(f32[128,2]{0,1:T(2,128)} %param.8) | data formatting | bytes 2048 | tf_op args[2]
  2.8 107.7 %shard_map.64 = bf16[128,1536]{1,0:T(8,128)(2,1)} custom-call(bf16[128,1536]{1,0:T(8,128)(2,1)} %tok_ref.1, s32[128,2]{1,0:T(8,128)} %copy.7.ids_ref, f32[128,2]{1,0:T(8,128)} %copy.8.rw_ref, bf16[2,1536,512]{2,1,0:T(8,128)(2,1)} %wg_hbm.1, bf16[2,1536,512]{2,1,0:T(8,128)(2,1)} %wu_hbm.1, bf16[2,512,1536]{2,1,0:T(8,128)(2,1)} %wd_hbm.1), custom_call_target="tpu_custom_call" | custom-call | tf_op jit(solution)/shard_map/pallas_call | solution.py:378
  110.5 1.8 %copy.10 = bf16[128,1536]{1,0:T(8,128)(2,1)} copy(bf16[128,1536]{1,0:T(8,128)(2,1)} %shard_map.64) | data formatting | bytes 786432

commit v2 on v0

v2 whole, which is shorter than its diff:
```python
import functools

import jax
import jax.numpy as jnp
from jax import lax
from jax.experimental import pallas as pl
from jax.experimental.pallas import tpu as pltpu
from jax.sharding import PartitionSpec as P

MESH = pl.DeviceIdType.MESH
CAP = 48
NZ, NY, NX = 8, 4, 4
UNITS = 16
SUB = 2
CUT = 3

STEPS = [
    128, 97, 4, 8, 5, 9, 96, 192, 160, 136, 16, 12, 256, 132, 17, 41,
    13, 144, 224, 140, 40, 20, 24, 168, 200, 21, 196, 25, 36, 148, 49, 152,
    204, 37, 28, 208, 29, 48, 156, 57, 164, 216, 176, 56, 220, 212, 61, 44,
    272, 280, 60, 45, 284, 188, 276, 268, 260, 172, 408, 184, 412, 52, 400, 472,
    53, 476, 477, 384, 404, 473, 252, 478, 264, 474, 180, 468, 396, 240, 469, 464,
    316, 470, 465, 466, 248, 460, 288, 392, 244, 304, 388, 461, 236, 444, 456, 452,
    312, 462, 508, 308, 232, 509, 453, 510, 228, 432, 457, 448, 458, 300, 416, 454,
    440, 436, 296, 504, 292, 500, 505, 449, 501, 428, 502, 496, 506, 450, 492, 424,
    420, 493, 497, 488, 484, 498, 494, 485, 489, 480, 490, 486, 481, 482, 320, 320,
]
FIRST = {n: next((code // 4) % 8 for code in STEPS if code // 32 == n) for n in (4, 5, 12, 13)}
WORDS = [
    sum(code << (9 * n) for n, code in enumerate(STEPS[at : at + 3])) for at in range(0, len(STEPS), 3)
]

F32, BF16 = jnp.float32, jnp.bfloat16


def dot(a, b, precision=None):
    return lax.dot_general(
        a, b, (((1,), (0,)), ((), ())), precision=precision, preferred_element_type=F32
    )


def down_rows(row, lanes):
    return jnp.broadcast_to(jnp.broadcast_to(row, (128, 128)).T[:, 0:1], (128, lanes))


def slot_hits(first_id, second_id, expert_of, slot_of):
    rows = first_id.shape[0]
    first, second = first_id == expert_of, second_id == expert_of
    named = jnp.where(first | second, 1.0, 0.0)
    earlier = lax.broadcasted_iota(jnp.int32, (rows, rows), 1) < lax.broadcasted_iota(
        jnp.int32, (rows, rows), 0
    )
    position = dot(jnp.where(earlier, 1.0, 0.0).astype(BF16), named.astype(BF16))
    here = position == slot_of.astype(F32)
    return first, second, jnp.where(here, named, 0.0)


def kernel(
    tok_ref, ids_ref, rw_ref, wg_hbm, wu_hbm, wd_hbm, out_ref,
    wg, wu, wd, xs, part, s_out, s_in, hid, own, pair_out, pair_in,
    c_out, c_in, eo0, eo1, comb, early,
    w_sem, a_ss, a_rs, p_ss, p_rs, x_ss, x_rs, q_ss, q_rs, c_ss, c_rs, y_ss, y_rs,
):
    dp, y, x = lax.axis_index("dp"), lax.axis_index("expert"), lax.axis_index("blk")
    z, c = dp // 2, dp % 2
    width = tok_ref.shape[1]
    sub_w, cut_w = width // SUB, width // CUT
    partner = (z * 2 + (1 - c), y, x)
    right, left, far = (dp, y, (x + 1) % NX), (dp, y, (x + NX - 1) % NX), (dp, y, (x + 2) % NX)
    q_right, q_left, q_far = (x + 1) % NX, (x + NX - 1) % NX, (x + 2) % NX

    def zdev(step):
        return (((z + step + NZ) % NZ) * 2 + c, y, x)

    def ydev(step):
        return (dp, (y + step) % NY, x)

    def zchip(i):
        k = (i + 1) // 2
        return (z + k * (1 - 2 * (i % 2)) + NZ) % NZ

    def remote(src, dst, ss, rs, dev):
        return pltpu.make_async_remote_copy(
            src_ref=src, dst_ref=dst, send_sem=ss, recv_sem=rs, device_id=dev, device_id_type=MESH
        )

    weights = [
        pltpu.make_async_copy(h.at[e], v.at[e], w_sem.at[n, e])
        for e in range(2)
        for n, (h, v) in enumerate(((wg_hbm, wg), (wu_hbm, wu), (wd_hbm, wd)))
    ]
    for w in weights:
        w.start()

    barrier = pltpu.get_barrier_semaphore()
    peers = [partner, zdev(1), zdev(-1), right, left, far, ydev(1), ydev(2), ydev(3)]
    for d in peers:
        pl.semaphore_signal(barrier, inc=1, device_id=d, device_id_type=MESH)

    ids = ids_ref[...].astype(F32)
    id_a, id_b = down_rows(ids[0:1], 128), down_rows(ids[1:2], 128)
    lane = lax.broadcasted_iota(jnp.int32, (128, 128), 1)
    for e in range(2):
        _, _, hit = slot_hits(id_a, id_b, (2 * y + e).astype(F32), lane)
        rows = lax.dot_general(
            hit.astype(BF16), tok_ref[...], (((0,), (0,)), ((), ())), preferred_element_type=F32
        )[:CAP].astype(BF16)
        for s in range(SUB):
            xs[e, s, dp] = rows[:, s * sub_w : (s + 1) * sub_w]
    pl.semaphore_wait(barrier, len(peers))

    def a_copy(e, s, chip, i, up):
        at = xs.at[e, s, 2 * chip + c]
        return remote(at, at, a_ss.at[e, up, s], a_rs.at[e, i, s], zdev(2 * up - 1))

    def p_copy(e, s, chip, i, core):
        at = xs.at[e, s, 2 * chip + core]
        return remote(at, at, p_ss.at[e, s], p_rs.at[e, i, s], partner)

    def send_own(e, s):
        a_copy(e, s, z, 1, 1).start()
        a_copy(e, s, z, 2, 0).start()
        p_copy(e, s, z, 0, c).start()

    def pass_on(e, i, s):
        chip = zchip(i)
        a_copy(e, s, chip, i, 1).wait_recv()

        @pl.when((i < 5) | (i + e == 5) | (i * e == 6))
        def _():
            on = a_copy(e, s, chip, i + 2 - i // 6, i % 2)
            on.wait_send()
            on.start()

        pair = p_copy(e, s, chip, i, c)
        pair.wait_send()
        pair.start()

    def x_copy(v, n):
        d = n % 2
        if n < 2:
            src, dst, way, sem = s_out.at[v, d, 0:2], s_in.at[v, d, 0:2], (right, left)[d], d
        elif n < 4:
            src, dst, way, sem = s_out.at[v, d, 2], s_in.at[v, d, 2], (right, left)[d], 2 + d
        else:
            src, dst, way, sem = hid.at[v, x], hid.at[v, x], (right, left, far)[n - 4], (0, 1, 4)[n - 4]
        return remote(src, dst, x_ss.at[v, (0, 1, 0, 1, 0, 1, 2)[n]], x_rs.at[v, sem], way)

    def x_landed(v, n):
        d = n % 2
        if n < 2:
            at, sem = s_in.at[v, d, 0:2], d
        elif n < 4:
            at, sem = s_in.at[v, d, 2], 2 + d
        else:
            at, sem = hid.at[v, (q_left, q_right, q_far)[n - 4]], (0, 1, 4)[n - 4]
        remote(at, at, x_ss.at[v, 0], x_rs.at[v, sem], right).wait_recv()

    def first(e, i):
        v = e * 8 + i
        chip = zchip(i)

        @pl.when((i == FIRST[4]) & (e == 0))
        def _():
            for n in range(2):
                weights[n].wait()

        @pl.when((i == FIRST[5]) & (e == 1))
        def _():
            for n in range(2):
                weights[3 + n].wait()

        for s in range(SUB):
            p_copy(e, s, chip, i, 1 - c).wait_recv()
        rows = [xs[e, s, pl.ds(2 * chip, 2)].reshape(2 * CAP, sub_w) for s in range(SUB)]
        for g, w in enumerate((wg, wu)):
            total = sum(dot(rows[s], w[e, s * sub_w : (s + 1) * sub_w]) for s in range(SUB))
            for q in range(NX):
                block = total[:, q * 128 : (q + 1) * 128]
                for h in range(2):
                    part[v, q, h, g] = block[h * CAP : (h + 1) * CAP]
        for d, near in enumerate((q_right, q_left)):
            s_out[v, d, 0] = part[v, q_far, d].astype(BF16)
            s_out[v, d, 1] = part[v, near, 1 - d].astype(BF16)
            x_copy(v, d).start()

    def second(e, i):
        v = e * 8 + i
        for d in range(2):
            x_landed(v, d)
        for d, near in enumerate((q_right, q_left)):
            s_out[v, d, 2] = (part[v, near, d] + s_in[v, d, 0].astype(F32)).astype(BF16)
            x_copy(v, d).wait_send()
            x_copy(v, 2 + d).start()

    def third(e, i):
        v = e * 8 + i
        for d in range(2):
            x_landed(v, 2 + d)
        for h in range(2):
            both = part[v, x, h] + s_in[v, h, 2].astype(F32) + s_in[v, 1 - h, 1].astype(F32)
            gate, up = both[0], both[1]
            hid[v, x, h] = (gate / (1.0 + jnp.exp(-gate)) * up).astype(BF16)
        for d in range(2):
            x_copy(v, 2 + d).wait_send()
        for n in range(4, 7):
            x_copy(v, n).start()

    def q_copy(v):
        return remote(pair_out.at[v], pair_in.at[v], q_ss.at[v], q_rs.at[v], partner)

    def sixth(e, i):
        v = e * 8 + i

        @pl.when((i == FIRST[12]) & (e == 0))
        def _():
            weights[2].wait()

        @pl.when((i == FIRST[13]) & (e == 1))
        def _():
            weights[5].wait()

        for n in range(4, 7):
            x_landed(v, n)
        rows = jnp.concatenate(
            [
                jnp.concatenate([hid[v, q, h] for q in range(NX)], axis=1)
                for h in (c, 1 - c)
            ],
            axis=0,
        )
        for n in range(CUT):
            block = dot(rows, wd[e, :, n * cut_w : (n + 1) * cut_w])
            own[v, n] = block[:CAP]
            pair_out[v, n] = block[CAP:]
        q_copy(v).start()
        for n in range(4, 7):
            x_copy(v, n).wait_send()

    def c_copy(e, i, n, up):
        v = e * 8 + i
        return remote(c_out.at[v, n], c_in.at[v, n], c_ss.at[e, up, n], c_rs.at[v, n], zdev(2 * up - 1))

    def y_copy(e, n, o):
        at = (eo0, eo1)[e].at[n, y]
        return remote(at, at, y_ss.at[e, n, o], y_rs.at[e, n, o], ydev(o))

    def y_landed(e, n, o):
        at = (eo0, eo1)[e].at[n, (y + NY - o) % NY]
        remote(at, at, y_ss.at[e, n, o], y_rs.at[e, n, o], ydev(o)).wait_recv()

    def reduce_z(e, i, n):
        v = e * 8 + i
        up = (1 - i % 2) + (i // 7) * e
        no_up = (i == 7) | (i + e == 6)

        @pl.when(n == 0)
        def _():
            q_copy(v).wait_recv()

        def from_up(slot):
            c_copy(e, slot, n, 0).wait_recv()
            return c_in[e * 8 + slot, n].astype(F32)

        @pl.when(no_up)
        def _():
            c_out[v, n] = (own[v, n] + pair_in[v, n]).astype(BF16)

        @pl.when((i > 0) & jnp.logical_not(no_up))
        def _():
            c_out[v, n] = (own[v, n] + pair_in[v, n] + from_up(i + 2 - i // 6)).astype(BF16)
            c_copy(e, i, n, up).wait_send()

        @pl.when(i > 0)
        def _():
            c_copy(e, i, n, up).start()

        @pl.when(i == 0)
        def _():
            total = own[v, n] + pair_in[v, n] + from_up(1) + from_up(2)
            for k in range(2):

                @pl.when(e == k)
                def _():
                    buf = (eo0, eo1)[k]
                    buf[n, y] = total.astype(buf.dtype)
                    for o in range(1, NY):
                        y_copy(k, n, o).start()

    for s in range(SUB):
        send_own(0, s)

    lanes = NY * CAP
    slot = lax.broadcasted_iota(jnp.int32, (128, lanes), 1)
    wide_a, wide_b = down_rows(ids[0:1], lanes), down_rows(ids[1:2], lanes)
    weight_a, weight_b = down_rows(rw_ref[0:1], lanes), down_rows(rw_ref[1:2], lanes)
    for e in range(2):
        expert_of = 2 * (slot // CAP) + e
        one, two, hit = slot_hits(wide_a, wide_b, expert_of.astype(F32), slot % CAP)
        weight = jnp.where(one, weight_a, 0.0) + jnp.where(two, weight_b, 0.0)
        comb[e] = weight * hit

    kinds = (
        pass_on,
        lambda e, i, s: send_own(e, s),
        lambda e, i, s: first(e, i),
        lambda e, i, s: second(e, i),
        lambda e, i, s: third(e, i),
        lambda e, i, s: None,
        lambda e, i, s: sixth(e, i),
        reduce_z,
    )

    def three(t, carry):
        word = jnp.int32(WORDS[-1])
        for n, value in enumerate(WORDS[:-1]):
            word = jnp.where(t == n, jnp.int32(value), word)

        def one(k, word):
            code = word & 511
            kind, e, i, s = code // 64, (code // 32) % 2, (code // 4) % 8, code % 4
            for n, step in enumerate(kinds):
                if n == 5:
                    continue

                @pl.when(kind == n)
                def _():
                    step(e, i, s)

            return word // 512

        lax.fori_loop(0, 3, one, word)
        return carry

    assert len(STEPS) % 3 == 0
    lax.fori_loop(0, len(WORDS), three, 0)

    for n in range(CUT):
        for o in range(1, NY):
            y_landed(0, n, o)
        early[n] = dot(comb[0], eo0[n].reshape(lanes, cut_w), lax.Precision.HIGHEST)

    for e in range(2):

        def sent(i, carry):
            q_copy(e * 8 + i).wait_send()
            return carry

        lax.fori_loop(0, 8, sent, 0)
        for up in range(2):
            for n in range(CUT):
                c_copy(e, 1, n, up).wait_send()
            for s in range(SUB):
                a_copy(e, s, z, 1, up).wait_send()
        for s in range(SUB):
            p_copy(e, s, z, 0, c).wait_send()
    for n in range(CUT):
        for o in range(1, NY):
            y_copy(0, n, o).wait_send()

    high = comb[1].astype(BF16)
    low = (comb[1] - high.astype(F32)).astype(BF16)
    for n in range(CUT):
        for o in range(1, NY):
            y_landed(1, n, o)
        late = eo1[n].reshape(lanes, cut_w)
        out_ref[:, n * cut_w : (n + 1) * cut_w] = (
            early[n] + dot(high, late) + dot(low, late)
        ).astype(BF16)
    for n in range(CUT):
        for o in range(1, NY):
            y_copy(1, n, o).wait_send()


def local(tokens, expert_ids, route_weights, gate_weight, up_weight, down_weight):
    rows, width = tokens.shape
    hidden = gate_weight.shape[2]
    quarter = hidden // NX
    vmem = pl.BlockSpec(memory_space=pltpu.VMEM)
    hbm = pl.BlockSpec(memory_space=pl.ANY)
    dma = pltpu.SemaphoreType.DMA
    return pl.pallas_call(
        kernel,
        out_shape=jax.ShapeDtypeStruct((rows, width), BF16),
        in_specs=[vmem, vmem, vmem, hbm, hbm, hbm],
        out_specs=vmem,
        scratch_shapes=[
            pltpu.VMEM(gate_weight.shape, BF16),
            pltpu.VMEM(up_weight.shape, BF16),
            pltpu.VMEM(down_weight.shape, BF16),
            pltpu.VMEM((2, SUB, 2 * NZ, CAP, width // SUB), BF16),
            pltpu.VMEM((UNITS, NX, 2, 2, CAP, quarter), F32),
            pltpu.VMEM((UNITS, 2, 3, 2, CAP, quarter), BF16),
            pltpu.VMEM((UNITS, 2, 3, 2, CAP, quarter), BF16),
            pltpu.VMEM((UNITS, NX, 2, CAP, quarter), BF16),
            pltpu.VMEM((UNITS, CUT, CAP, width // CUT), F32),
            pltpu.VMEM((UNITS, CUT, CAP, width // CUT), F32),
            pltpu.VMEM((UNITS, CUT, CAP, width // CUT), F32),
            pltpu.VMEM((UNITS, CUT, CAP, width // CUT), BF16),
            pltpu.VMEM((UNITS, CUT, CAP, width // CUT), BF16),
            pltpu.VMEM((CUT, NY, CAP, width // CUT), F32),
            pltpu.VMEM((CUT, NY, CAP, width // CUT), BF16),
            pltpu.VMEM((2, rows, NY * CAP), F32),
            pltpu.VMEM((CUT, rows, width // CUT), F32),
            dma((3, 2)),
            dma((2, 2, SUB)),
            dma((2, 8, SUB)),
            dma((2, SUB)),
            dma((2, 8, SUB)),
            dma((UNITS, 3)),
            dma((UNITS, 5)),
            dma((UNITS,)),
            dma((UNITS,)),
            dma((2, 2, CUT)),
            dma((UNITS, CUT)),
            dma((2, CUT, NY)),
            dma((2, CUT, NY)),
        ],
        compiler_params=pltpu.CompilerParams(
            collective_id=0, has_side_effects=True, vmem_limit_bytes=60 * 2**20
        ),
    )(tokens, expert_ids.T, route_weights.T, gate_weight, up_weight, down_weight)


def solution(mesh):
    placed = (
        P("dp", "blk"),
        P("dp", None),
        P("dp", None),
        P("expert", "blk", "dp"),
        P("expert", "blk", "dp"),
        P("expert", "dp", "blk"),
    )
    return jax.shard_map(
        local, mesh=mesh, in_specs=placed, out_specs=P("dp", "blk"), check_vma=False
    )
```

time: 316 us -> 86.2 us (0.27); the launches traced: 311 us -> 86.1 us
  waiting for transfers between devices: 247 us -> 0 us
  Pallas kernels: 0 us -> 84.3 us
  blocking collectives: 23.4 us -> 0 us
  matrix products: 20.9 us -> 0 us
  between operations: 13.2 us -> 0.01 us
  other arithmetic: 4.85 us -> 0 us
    psum x1 -> x0, waiting for transfers between devices: 130 us -> none  [local(): summed = lax.psum(partial_value, 'blk')]
    pallas_call x0 -> x1, Pallas kernels: none -> 84.3 us  [local(): pl.pallas_call(kernel, out_shape=jax.ShapeDtypeStruct((rows, width), BF16...]
    reduce_scatter x1 -> x0, waiting for transfers between devices: 69.2 us -> none  [local(): lax.psum_scatter(jnp.einsum('enh,ehd->ned', hidden, down_weight, preferre...]
    all_gather x1 -> x0, waiting for transfers between devices: 47.1 us -> none  [local(): shard_rows = lax.all_gather(picked, 'dp', axis=1, tiled=True)]
    psum x1 -> x0, blocking collectives: 23.4 us -> none  [local(): mixed = lax.psum(mixed_part, 'expert')]
    dot_general x5 -> x0, matrix products: 20.9 us -> none  [the longest x1 8.04 us: local(): jnp.einsum('enh,ehd->ned', hidden, down_weight, preferred_element_type=jn...]
    another operation x3 -> x0, other arithmetic: 4 us -> none  [the longest x1 3.37 us: local(): partial_value = jnp.stack([gate_part, up_part])]
  transfers between devices with their start and end apart: 3 -> 0, of which waited for: 3 -> 0; matrix products, arithmetic and copies ran while one was open for 0% -> 0% of each run, Pallas kernels for 0% -> 0%
where the time goes in v2:
time: 86.2 us; the launch traced here: 86.1 us
  Pallas kernels  84.3 us (98%)
  local copies, waits for them, and re-layouts  1.77 us (2%)
    pallas_call x1, Pallas kernels, local(): pl.pallas_call(kernel, out_shape=jax.ShapeDtypeStruct((rows, width), BF16...  84.3 us
    unnamed x1, local copies, waits for them, and re-layouts  1.77 us

profile of v2, /device:TPU:1, one launch (start us, length us, event | category | flops | bytes accessed | tf_op | source)
XLA Modules:
  0.0 86.1 jit_solution(14365588404727491245)
XLA Ops:
  0.0 84.3 %shard_map.64 = bf16[128,1536]{1,0:T(8,128)(2,1)} custom-call(bf16[128,1536]{1,0:T(8,128)(2,1)} %tok_ref.1, s32[2,128]{1,0:T(2,128)} %bitcast.2, f32[2,128]{1,0:T(2,128)} %bitcast.3, bf16[2,1536,512]{2,1,0:T(8,128)(2,1)} %wg_hbm.1, bf16[2,1536,512]{2,1,0:T(8,128)(2,1)} %wu_hbm.1, bf16[2,512,1536]{2,1,0:T(8,128)(2,1)} %wd_hbm.1), custom_call_target="tpu_custom_call" | custom-call | tf_op jit(solution)/shard_map/pallas_call | solution.py:382
  84.3 1.8 %copy.8 = bf16[128,1536]{1,0:T(8,128)(2,1)} copy(bf16[128,1536]{1,0:T(8,128)(2,1)} %shard_map.64) | data formatting | bytes 786432

commit v3 on v2

--- a/solution.py
+++ b/solution.py
@@ -15,15 +15,15 @@
 CUT = 3
 
 STEPS = [
-    128, 97, 4, 8, 5, 9, 96, 192, 160, 136, 16, 12, 256, 132, 17, 41,
-    13, 144, 224, 140, 40, 20, 24, 168, 200, 21, 196, 25, 36, 148, 49, 152,
-    204, 37, 28, 208, 29, 48, 156, 57, 164, 216, 176, 56, 220, 212, 61, 44,
-    272, 280, 60, 45, 284, 188, 276, 268, 260, 172, 408, 184, 412, 52, 400, 472,
-    53, 476, 477, 384, 404, 473, 252, 478, 264, 474, 180, 468, 396, 240, 469, 464,
-    316, 470, 465, 466, 248, 460, 288, 392, 244, 304, 388, 461, 236, 444, 456, 452,
-    312, 462, 508, 308, 232, 509, 453, 510, 228, 432, 457, 448, 458, 300, 416, 454,
-    440, 436, 296, 504, 292, 500, 505, 449, 501, 428, 502, 496, 506, 450, 492, 424,
-    420, 493, 497, 488, 484, 498, 494, 485, 489, 480, 490, 486, 481, 482, 320, 320,
+    128, 96, 4, 8, 9, 5, 97, 192, 136, 132, 12, 160, 16, 256, 17, 13,
+    40, 200, 144, 140, 196, 41, 20, 168, 21, 25, 36, 24, 264, 208, 152, 28,
+    148, 29, 48, 37, 204, 156, 49, 44, 216, 164, 45, 212, 384, 56, 220, 57,
+    52, 272, 280, 392, 53, 284, 180, 276, 60, 184, 61, 408, 188, 412, 472, 473,
+    244, 268, 476, 477, 478, 172, 404, 400, 252, 260, 474, 468, 176, 464, 465, 469,
+    396, 248, 316, 224, 460, 308, 470, 236, 466, 388, 461, 240, 228, 312, 456, 457,
+    452, 444, 462, 232, 508, 458, 436, 453, 300, 448, 304, 509, 500, 501, 440, 510,
+    502, 292, 504, 449, 454, 296, 428, 432, 505, 492, 288, 496, 493, 494, 420, 506,
+    424, 450, 497, 484, 488, 485, 498, 416, 486, 489, 480, 490, 481, 482, 320, 320,
 ]
 FIRST = {n: next((code // 4) % 8 for code in STEPS if code // 32 == n) for n in (4, 5, 12, 13)}
 WORDS = [
@@ -115,7 +115,7 @@
 
     def p_copy(e, s, chip, i, core):
         at = xs.at[e, s, 2 * chip + core]
-        return remote(at, at, p_ss.at[e, s], p_rs.at[e, i, s], partner)
+        return remote(at, at, p_ss.at[e, s], p_rs.at[e, i], partner)
 
     def send_own(e, s):
         a_copy(e, s, z, 1, 1).start()
@@ -139,22 +139,16 @@
     def x_copy(v, n):
         d = n % 2
         if n < 2:
-            src, dst, way, sem = s_out.at[v, d, 0:2], s_in.at[v, d, 0:2], (right, left)[d], d
+            at, way, stage = (s_out.at[v, d, 0:2], s_in.at[v, d, 0:2]), (right, left)[d], 0
         elif n < 4:
-            src, dst, way, sem = s_out.at[v, d, 2], s_in.at[v, d, 2], (right, left)[d], 2 + d
+            at, way, stage = (s_out.at[v, d, 2], s_in.at[v, d, 2]), (right, left)[d], 1
         else:
-            src, dst, way, sem = hid.at[v, x], hid.at[v, x], (right, left, far)[n - 4], (0, 1, 4)[n - 4]
-        return remote(src, dst, x_ss.at[v, (0, 1, 0, 1, 0, 1, 2)[n]], x_rs.at[v, sem], way)
-
-    def x_landed(v, n):
-        d = n % 2
-        if n < 2:
-            at, sem = s_in.at[v, d, 0:2], d
-        elif n < 4:
-            at, sem = s_in.at[v, d, 2], 2 + d
-        else:
-            at, sem = hid.at[v, (q_left, q_right, q_far)[n - 4]], (0, 1, 4)[n - 4]
-        remote(at, at, x_ss.at[v, 0], x_rs.at[v, sem], right).wait_recv()
+            at, way, stage = (hid.at[v, x], hid.at[v, x]), (right, left, far)[n - 4], 2
+        return remote(*at, x_ss.at[v], x_rs.at[v, stage], way)
+
+    def x_all(v, stage):
+        at = (s_in.at[v, :, 0:2], s_in.at[v, :, 2], hid.at[v, 0:3])[stage]
+        return remote(at, at, x_ss.at[v], x_rs.at[v, stage], right)
 
     def first(e, i):
         v = e * 8 + i
@@ -170,8 +164,8 @@
             for n in range(2):
                 weights[3 + n].wait()
 
-        for s in range(SUB):
-            p_copy(e, s, chip, i, 1 - c).wait_recv()
+        at = xs.at[e, :, 2 * chip + 1 - c]
+        remote(at, at, p_ss.at[e, 0], p_rs.at[e, i], partner).wait_recv()
         rows = [xs[e, s, pl.ds(2 * chip, 2)].reshape(2 * CAP, sub_w) for s in range(SUB)]
         for g, w in enumerate((wg, wu)):
             total = sum(dot(rows[s], w[e, s * sub_w : (s + 1) * sub_w]) for s in range(SUB))
@@ -186,28 +180,23 @@
 
     def second(e, i):
         v = e * 8 + i
-        for d in range(2):
-            x_landed(v, d)
+        x_all(v, 0).wait()
         for d, near in enumerate((q_right, q_left)):
             s_out[v, d, 2] = (part[v, near, d] + s_in[v, d, 0].astype(F32)).astype(BF16)
-            x_copy(v, d).wait_send()
             x_copy(v, 2 + d).start()
 
     def third(e, i):
         v = e * 8 + i
-        for d in range(2):
-            x_landed(v, 2 + d)
+        x_all(v, 1).wait()
         for h in range(2):
             both = part[v, x, h] + s_in[v, h, 2].astype(F32) + s_in[v, 1 - h, 1].astype(F32)
             gate, up = both[0], both[1]
             hid[v, x, h] = (gate / (1.0 + jnp.exp(-gate)) * up).astype(BF16)
-        for d in range(2):
-            x_copy(v, 2 + d).wait_send()
         for n in range(4, 7):
             x_copy(v, n).start()
 
     def q_copy(v):
-        return remote(pair_out.at[v], pair_in.at[v], q_ss.at[v], q_rs.at[v], partner)
+        return remote(pair_out.at[v], pair_in.at[v], q_ss.at[0], q_rs.at[v], partner)
 
     def sixth(e, i):
         v = e * 8 + i
@@ -220,8 +209,7 @@
         def _():
             weights[5].wait()
 
-        for n in range(4, 7):
-            x_landed(v, n)
+        x_all(v, 2).wait()
         rows = jnp.concatenate(
             [
                 jnp.concatenate([hid[v, q, h] for q in range(NX)], axis=1)
@@ -234,8 +222,6 @@
             own[v, n] = block[:CAP]
             pair_out[v, n] = block[CAP:]
         q_copy(v).start()
-        for n in range(4, 7):
-            x_copy(v, n).wait_send()
 
     def c_copy(e, i, n, up):
         v = e * 8 + i
@@ -243,11 +229,15 @@
 
     def y_copy(e, n, o):
         at = (eo0, eo1)[e].at[n, y]
-        return remote(at, at, y_ss.at[e, n, o], y_rs.at[e, n, o], ydev(o))
-
-    def y_landed(e, n, o):
-        at = (eo0, eo1)[e].at[n, (y + NY - o) % NY]
-        remote(at, at, y_ss.at[e, n, o], y_rs.at[e, n, o], ydev(o)).wait_recv()
+        return remote(at, at, y_ss.at[e], y_rs.at[e, n], ydev(o))
+
+    def y_all(e, n):
+        at = (eo0, eo1)[e].at[n, 1:NY]
+        return remote(at, at, y_ss.at[e], y_rs.at[e, n], ydev(1))
+
+    def y_sent(e):
+        at = (eo0, eo1)[e].at[:, 1:NY]
+        remote(at, at, y_ss.at[e], y_rs.at[e, 0], ydev(1)).wait_send()
 
     def reduce_z(e, i, n):
         v = e * 8 + i
@@ -289,16 +279,6 @@
 
     for s in range(SUB):
         send_own(0, s)
-
-    lanes = NY * CAP
-    slot = lax.broadcasted_iota(jnp.int32, (128, lanes), 1)
-    wide_a, wide_b = down_rows(ids[0:1], lanes), down_rows(ids[1:2], lanes)
-    weight_a, weight_b = down_rows(rw_ref[0:1], lanes), down_rows(rw_ref[1:2], lanes)
-    for e in range(2):
-        expert_of = 2 * (slot // CAP) + e
-        one, two, hit = slot_hits(wide_a, wide_b, expert_of.astype(F32), slot % CAP)
-        weight = jnp.where(one, weight_a, 0.0) + jnp.where(two, weight_b, 0.0)
-        comb[e] = weight * hit
 
     kinds = (
         pass_on,
@@ -335,18 +315,23 @@
     assert len(STEPS) % 3 == 0
     lax.fori_loop(0, len(WORDS), three, 0)
 
+    lanes = NY * CAP
+    slot = lax.broadcasted_iota(jnp.int32, (128, lanes), 1)
+    wide_a, wide_b = down_rows(ids[0:1], lanes), down_rows(ids[1:2], lanes)
+    weight_a, weight_b = down_rows(rw_ref[0:1], lanes), down_rows(rw_ref[1:2], lanes)
+    for e in range(2):
+        expert_of = 2 * (slot // CAP) + e
+        one, two, hit = slot_hits(wide_a, wide_b, expert_of.astype(F32), slot % CAP)
+        weight = jnp.where(one, weight_a, 0.0) + jnp.where(two, weight_b, 0.0)
+        comb[e] = weight * hit
+
     for n in range(CUT):
-        for o in range(1, NY):
-            y_landed(0, n, o)
+        y_all(0, n).wait_recv()
         early[n] = dot(comb[0], eo0[n].reshape(lanes, cut_w), lax.Precision.HIGHEST)
 
+    remote(pair_out, pair_in, q_ss.at[0], q_rs.at[0], partner).wait_send()
     for e in range(2):
 
-        def sent(i, carry):
-            q_copy(e * 8 + i).wait_send()
-            return carry
-
-        lax.fori_loop(0, 8, sent, 0)
         for up in range(2):
             for n in range(CUT):
                 c_copy(e, 1, n, up).wait_send()
@@ -354,22 +339,17 @@
                 a_copy(e, s, z, 1, up).wait_send()
         for s in range(SUB):
             p_copy(e, s, z, 0, c).wait_send()
-    for n in range(CUT):
-        for o in range(1, NY):
-            y_copy(0, n, o).wait_send()
+    y_sent(0)
 
     high = comb[1].astype(BF16)
     low = (comb[1] - high.astype(F32)).astype(BF16)
     for n in range(CUT):
-        for o in range(1, NY):
-            y_landed(1, n, o)
+        y_all(1, n).wait_recv()
         late = eo1[n].reshape(lanes, cut_w)
         out_ref[:, n * cut_w : (n + 1) * cut_w] = (
             early[n] + dot(high, late) + dot(low, late)
         ).astype(BF16)
-    for n in range(CUT):
-        for o in range(1, NY):
-            y_copy(1, n, o).wait_send()
+    y_sent(1)
 
 
 def local(tokens, expert_ids, route_weights, gate_weight, up_weight, down_weight):
@@ -406,15 +386,15 @@
             dma((2, 2, SUB)),
             dma((2, 8, SUB)),
             dma((2, SUB)),
-            dma((2, 8, SUB)),
+            dma((2, 8)),
+            dma((UNITS,)),
             dma((UNITS, 3)),
-            dma((UNITS, 5)),
-            dma((UNITS,)),
+            dma((1,)),
             dma((UNITS,)),
             dma((2, 2, CUT)),
             dma((UNITS, CUT)),
-            dma((2, CUT, NY)),
-            dma((2, CUT, NY)),
+            dma((2,)),
+            dma((2, CUT)),
         ],
         compiler_params=pltpu.CompilerParams(
             collective_id=0, has_side_effects=True, vmem_limit_bytes=60 * 2**20

time: 86.2 us -> 84.1 us (0.976)
  Pallas kernels: 84.3 us -> 82.2 us
    pallas_call x1, Pallas kernels: 84.3 us -> 82.2 us  [local(): pl.pallas_call(kernel, out_shape=jax.ShapeDtypeStruct((rows, width), BF16...]
where the time goes in v3:
time: 84.1 us; the launch traced here: 84 us
  Pallas kernels  82.2 us (98%)
  local copies, waits for them, and re-layouts  1.77 us (2%)
    pallas_call x1, Pallas kernels, local(): pl.pallas_call(kernel, out_shape=jax.ShapeDtypeStruct((rows, width), BF16...  82.2 us
    unnamed x1, local copies, waits for them, and re-layouts  1.77 us

profile of v3, /device:TPU:1, one launch (start us, length us, event | category | flops | bytes accessed | tf_op | source)
XLA Modules:
  0.0 84.0 jit_solution(17609205069242074811)
XLA Ops:
  0.0 82.2 %shard_map.64 = bf16[128,1536]{1,0:T(8,128)(2,1)} custom-call(bf16[128,1536]{1,0:T(8,128)(2,1)} %tok_ref.1, s32[2,128]{1,0:T(2,128)} %bitcast.2, f32[2,128]{1,0:T(2,128)} %bitcast.3, bf16[2,1536,512]{2,1,0:T(8,128)(2,1)} %wg_hbm.1, bf16[2,1536,512]{2,1,0:T(8,128)(2,1)} %wu_hbm.1, bf16[2,512,1536]{2,1,0:T(8,128)(2,1)} %wd_hbm.1), custom_call_target="tpu_custom_call" | custom-call | tf_op jit(solution)/shard_map/pallas_call | solution.py:362
  82.2 1.8 %copy.8 = bf16[128,1536]{1,0:T(8,128)(2,1)} copy(bf16[128,1536]{1,0:T(8,128)(2,1)} %shard_map.64) | data formatting | bytes 786432

commit v4 on v3

--- a/solution.py
+++ b/solution.py
@@ -89,24 +89,25 @@
         for e in range(2)
         for n, (h, v) in enumerate(((wg_hbm, wg), (wu_hbm, wu), (wd_hbm, wd)))
     ]
-    for w in weights:
-        w.start()
 
     barrier = pltpu.get_barrier_semaphore()
     peers = [partner, zdev(1), zdev(-1), right, left, far, ydev(1), ydev(2), ydev(3)]
     for d in peers:
         pl.semaphore_signal(barrier, inc=1, device_id=d, device_id_type=MESH)
+    for w in weights:
+        w.start()
 
     ids = ids_ref[...].astype(F32)
     id_a, id_b = down_rows(ids[0:1], 128), down_rows(ids[1:2], 128)
     lane = lax.broadcasted_iota(jnp.int32, (128, 128), 1)
-    for e in range(2):
+    def pick(e):
         _, _, hit = slot_hits(id_a, id_b, (2 * y + e).astype(F32), lane)
         rows = lax.dot_general(
             hit.astype(BF16), tok_ref[...], (((0,), (0,)), ((), ())), preferred_element_type=F32
         )[:CAP].astype(BF16)
         for s in range(SUB):
             xs[e, s, dp] = rows[:, s * sub_w : (s + 1) * sub_w]
+    pick(0)
     pl.semaphore_wait(barrier, len(peers))
 
     def a_copy(e, s, chip, i, up):
@@ -279,6 +280,7 @@
 
     for s in range(SUB):
         send_own(0, s)
+    pick(1)
 
     kinds = (
         pass_on,

time: 84.1 us -> 84.1 us (level)
  no operation moved by 1% of the time
where the time goes in v4:
time: 84.1 us; the launch traced here: 84 us
  Pallas kernels  82.2 us (98%)
  local copies, waits for them, and re-layouts  1.77 us (2%)
    pallas_call x1, Pallas kernels, local(): pl.pallas_call(kernel, out_shape=jax.ShapeDtypeStruct((rows, width), BF16...  82.2 us
    unnamed x1, local copies, waits for them, and re-layouts  1.77 us

profile of v4, /device:TPU:1, one launch (start us, length us, event | category | flops | bytes accessed | tf_op | source)
XLA Modules:
  0.0 84.0 jit_solution(1009689315646642715)
XLA Ops:
  0.0 82.2 %shard_map.64 = bf16[128,1536]{1,0:T(8,128)(2,1)} custom-call(bf16[128,1536]{1,0:T(8,128)(2,1)} %tok_ref.1, s32[2,128]{1,0:T(2,128)} %bitcast.2, f32[2,128]{1,0:T(2,128)} %bitcast.3, bf16[2,1536,512]{2,1,0:T(8,128)(2,1)} %wg_hbm.1, bf16[2,1536,512]{2,1,0:T(8,128)(2,1)} %wu_hbm.1, bf16[2,512,1536]{2,1,0:T(8,128)(2,1)} %wd_hbm.1), custom_call_target="tpu_custom_call" | custom-call | tf_op jit(solution)/shard_map/pallas_call | solution.py:364
  82.2 1.8 %copy.8 = bf16[128,1536]{1,0:T(8,128)(2,1)} copy(bf16[128,1536]{1,0:T(8,128)(2,1)} %shard_map.64) | data formatting | bytes 786432
